TPU v7x, 32 devices: a whole 2x2x4 slice. The times are simulated.
32 devices in a mesh: groups: 2 (over y), loop: 4 (over z), enc: 2 (over x), rep: 2 (over core).
Axes of the slice: x: 2, y: 2, z: 4, core: 2. Of those that a mesh axis runs over, the one named last changes fastest.
Arguments:
- embeddings: bfloat16 [4096, 768], P(('groups', 'loop', 'rep'), 'enc'), parts along dimension 0, may hold values from -24 to 24
- head_weight: bfloat16 [768, 768], P('enc'), may hold values from -0.21875 to 0.21875
- gp_weights: float32 [4096], P('groups'), parts along dimension 0, may hold values from -24 to 24
- counts: int32 [8], P('groups'), parts along dimension 0, may hold values from 64 to 512, as said below
Outputs:
- embed_grad: bfloat16 [4096, 768], P(('groups', 'loop', 'rep'), 'enc'), parts along dimension 0
- head_grad: float32 [1536, 768], P(('groups', 'enc')), parts along dimension 0
There are 2 independent parts, one for each index of `groups`. A program takes and returns all parts, laid end to end along the dimension named above; an argument that names none is the same for every part. Nothing has to cross between parts.
Inputs may be any that keep to these rules, and one draw needn't show every extreme that they name: `counts`: some block is full and some block holds exactly 64 valid molecules.
All inputs are finite; a program needn't handle non-finite values.
Results may differ from a plain program's by a relative error of at most 0.019.
Values may be sent and summed in bfloat16 or wider, within the bound.
No kernel may reach another device: no remote copies, remote signals or barrier semaphores. Data moves between devices by JAX's collectives and lax.ppermute only.
A program may use at most 64 MiB of HBM per device.

v0:
```python
import jax
import jax.numpy as jnp
from jax import lax
from jax.sharding import PartitionSpec as P

EPSILON = 1e-06


def passed_along(value, axis, steps):
    count = lax.axis_size(axis)
    pairs = [(source, (source + steps) % count) for source in range(count)]
    return lax.ppermute(value, axis, pairs)


def pass_forward(piece):
    return passed_along(piece, "loop", 1)


def body(embeddings, head_weight, gp_weights, counts):
    enc_size = lax.axis_size("enc")
    rep_size = lax.axis_size("rep")
    loop_size = lax.axis_size("loop")
    share_rows = embeddings.shape[0]
    piece_rows = share_rows // enc_size
    block_rows = share_rows * rep_size
    loop_index = lax.axis_index("loop")
    enc_index = lax.axis_index("enc")
    rep_index = lax.axis_index("rep")
    rows = embeddings
    own_feats = lax.psum_scatter(
        jnp.dot(rows, head_weight, preferred_element_type=jnp.float32),
        "enc",
        scatter_dimension=0,
        tiled=True,
    ).astype(jnp.bfloat16)
    block_feats = lax.all_gather(own_feats, ("enc", "rep"), axis=0, tiled=True)
    block_norms = jnp.sum(jnp.square(block_feats.astype(jnp.float32)), axis=1)
    offsets = (
        jnp.arange(rep_size, dtype=jnp.int32)[None, :, None] * share_rows
        + jnp.arange(enc_size, dtype=jnp.int32)[:, None, None] * piece_rows
        + jnp.arange(piece_rows, dtype=jnp.int32)[None, None, :]
    ).reshape(block_rows)
    own_base = lax.dynamic_slice_in_dim(gp_weights, loop_index * block_rows, block_rows)
    block_coef = (
        own_base.reshape(rep_size, enc_size, piece_rows).transpose(1, 0, 2).reshape(block_rows)
    )
    own_count = lax.dynamic_index_in_dim(counts, loop_index, keepdims=False)
    block_coef = jnp.where(offsets < own_count, block_coef, 0.0)
    piece_start = rep_index * share_rows + enc_index * piece_rows
    piece_offsets = piece_start + jnp.arange(piece_rows, dtype=jnp.int32)

    def tile(state, piece, anchor):
        anchor_count = lax.dynamic_index_in_dim(counts, anchor, keepdims=False)
        accum, quotient_sum = state
        piece_coef = lax.dynamic_slice_in_dim(
            gp_weights, anchor * block_rows + piece_start, piece_rows
        )
        piece_coef = jnp.where(piece_offsets < anchor_count, piece_coef, 0.0)
        piece_norms = jnp.sum(jnp.square(piece.astype(jnp.float32)), axis=1)
        scores = lax.dot_general(
            piece, block_feats, (((1,), (1,)), ((), ())), preferred_element_type=jnp.float32
        )
        denom = piece_norms[:, None] + block_norms[None, :] - scores + EPSILON
        inverse = 1.0 / (denom * denom)
        pair_coef = piece_coef[:, None] * block_coef[None, :]
        pair_weight = (pair_coef * (piece_norms[:, None] + block_norms[None, :]) * inverse).astype(
            jnp.bfloat16
        )
        quotient_sum = quotient_sum + jnp.sum(pair_coef * 2.0 * scores * inverse, axis=0)
        accum = accum + lax.dot_general(
            pair_weight, piece, (((0,), (0,)), ((), ())), preferred_element_type=jnp.float32
        )
        return (accum, quotient_sum)

    start_state = (
        jnp.zeros((block_rows, block_feats.shape[1]), jnp.float32),
        jnp.zeros((block_rows,), jnp.float32),
    )
    state = tile(start_state, own_feats, loop_index)

    def forward_step(step_index, carry):
        moving, inner = carry
        moving = pass_forward(moving)
        inner = tile(inner, moving, (loop_index - step_index - 1 + loop_size) % loop_size)
        return (moving, inner)

    moving, state = lax.fori_loop(0, loop_size - 1, forward_step, (own_feats, state))
    accum, quotient_sum = state
    grad_block = accum - block_feats.astype(jnp.float32) * quotient_sum[:, None]
    own_grad = lax.psum_scatter(
        grad_block.astype(jnp.bfloat16), ("enc", "rep"), scatter_dimension=0, tiled=True
    )
    piece = lax.all_gather(own_grad, "enc", axis=0, tiled=True)
    back = lax.dot_general(
        piece, head_weight, (((1,), (1,)), ((), ())), preferred_element_type=jnp.float32
    )
    embed_part = back
    rows = embeddings
    head_part = lax.dot_general(
        rows, piece, (((0,), (0,)), ((), ())), preferred_element_type=jnp.float32
    )
    embed_part, head_part = (embed_part, head_part)
    head_grad = lax.psum(head_part, ("loop", "rep"))
    return (embed_part.astype(jnp.bfloat16), head_grad)


def solution(mesh):
    placed = (P(("groups", "loop", "rep"), "enc"), P("enc", None), P("groups"), P("groups"))
    return jax.shard_map(
        body,
        mesh=mesh,
        in_specs=placed,
        out_specs=(P(("groups", "loop", "rep"), "enc"), P(("groups", "enc"), None)),
        check_vma=False,
    )
```

profile of v0, /device:TPU:0, one launch (start us, length us, event | category | flops | bytes accessed | tf_op | source)
XLA Modules:
  0.0 170.0 jit_solution(11172648524668776611)
XLA Ops:
  7.2 0.0 reduce-scatter.3.cloned.1.call-start
  7.2 1.0 copy-done
  8.2 2.2 %fusion.40 = f32[256,768]{1,0:T(8,128)} fusion(bf16[256,384]{1,0:T(8,128)(2,1)} %param.6, bf16[384,768]{1,0:T(8,128)(2,1)S(1)} %copy-done), kind=kOutput, calls=%fused_computation.56 | convolution fusion | flops 150994944 | bytes 1572864 | tf_op jit(solution)/shard_map/dot_general | solution.py:31
  10.4 0.0 reduce-scatter.3.cloned.1.call-update
  10.4 0.0 reduce-scatter.5.cloned.1.call-start
  10.5 0.7 dynamic_slice.37
  11.2 0.8 dynamic_slice.39
  11.9 0.1 broadcast_add_fusion
  12.0 0.8 compare_select_fusion.1
  12.8 1.5 compare_select_fusion.2
  14.2 16.8 %reduce-scatter.3.cloned.1.call-done = f32[128,768]{1,0:T(8,128)} async-done(((f32[256,768]{1,0:T(8,128)}), f32[128,768]{1,0:T(8,128)}) %reduce-scatter.3.cloned.1.call-update) | async-done | bytes 393232 | tf_op jit(solution)/shard_map/reduce_scatter | solution.py:30
  31.0 1.1 multiply_reduce_fusion.1
  32.1 8.2 %all_gather.6 = bf16[512,768]{1,0:T(8,128)(2,1)S(1)} all-gather(bf16[128,768]{1,0:T(8,128)(2,1)S(1)} %get-tuple-element.541), channel_id=1, replica_groups=mesh['groups'=2,'loop'=4,'enc'=2,'rep'=2] {'enc','rep'}, dimensions={0}, use_global_device_ids=true | all-gather | bytes 983040 | tf_op jit(solution)/shard_map/all_gather | solution.py:36
  40.3 0.2 fusion.19
  40.6 0.4 fusion.24
  41.0 0.5 fusion.30
  41.5 28.3 %while.23 = (s32[]{:T(128)}, bf16[128,768]{1,0:T(8,128)(2,1)S(1)}, f32[512,768]{1,0:T(8,128)S(1)}, f32[512]{0:T(512)S(1)}, s32[]{:T(128)}, /*index=5*/s32[4]{0:T...) while((s32[]{:T(128)}, bf16[128,768]{1,0:T(8,128)(2,1)S(1)}, ...), condition=%wide.region_7.8_spmd.clone.clone, body=%wide.region_4.7_spmd.clone.clone.sunk | while | flops 203260192 | bytes 6246334 | solution.py:87
  41.5 1.5 collective-permute-start
  43.1 0.6 dynamic_slice.49
  43.6 1.4 compare_select_fusion.4
  45.1 5.5 %collective-permute-done = bf16[128,768]{1,0:T(8,128)(2,1)S(1)} collective-permute-done((bf16[128,768]{1,0:T(8,128)(2,1)S(1)}, bf16[128,768]{1,0:T(8,128)(2,1)S(1)}, u32[]{:S(2)}, u32[]{:S(2)}) %collective-permute-start) | collective-permute-done | bytes 196640 | tf_op jit(solution)/shard_map/while/body/eval_jaxpr/ppermute | solution.py:12
  50.5 0.1 multiply_reduce_fusion.3
  50.6 0.4 fusion.62
  51.1 0.6 convolution_add_fusion.2
  51.7 0.1 collective-permute-start
  51.8 0.6 dynamic_slice.49
  52.4 1.4 compare_select_fusion.4
  53.8 6.1 %collective-permute-done = bf16[128,768]{1,0:T(8,128)(2,1)S(1)} collective-permute-done((bf16[128,768]{1,0:T(8,128)(2,1)S(1)}, bf16[128,768]{1,0:T(8,128)(2,1)S(1)}, u32[]{:S(2)}, u32[]{:S(2)}) %collective-permute-start) | collective-permute-done | bytes 196640 | tf_op jit(solution)/shard_map/while/body/eval_jaxpr/ppermute | solution.py:12
  59.9 0.1 multiply_reduce_fusion.3
  60.0 0.4 fusion.62
  60.5 0.6 convolution_add_fusion.2
  61.1 0.1 collective-permute-start
  61.2 0.6 dynamic_slice.49
  61.8 1.4 compare_select_fusion.4
  63.2 5.4 %collective-permute-done = bf16[128,768]{1,0:T(8,128)(2,1)S(1)} collective-permute-done((bf16[128,768]{1,0:T(8,128)(2,1)S(1)}, bf16[128,768]{1,0:T(8,128)(2,1)S(1)}, u32[]{:S(2)}, u32[]{:S(2)}) %collective-permute-start) | collective-permute-done | bytes 196640 | tf_op jit(solution)/shard_map/while/body/eval_jaxpr/ppermute | solution.py:12
  68.6 0.1 multiply_reduce_fusion.3
  68.8 0.4 fusion.62
  69.2 0.6 convolution_add_fusion.2
  69.8 1.1 fusion.21
  71.0 0.0 reduce-scatter.5.cloned.1.call-update
  71.0 0.0 all-reduce.2.cloned.1.call-start
  71.1 20.9 %reduce-scatter.5.cloned.1.call-done = bf16[128,768]{1,0:T(8,128)(2,1)} async-done(((bf16[512,768]{1,0:T(8,128)(2,1)}), bf16[128,768]{1,0:T(8,128)(2,1)}) %reduce-scatter.5.cloned.1.call-update) | async-done | bytes 196624 | tf_op jit(solution)/shard_map/reduce_scatter | solution.py:90
  92.0 7.5 %all_gather.7 = bf16[256,768]{1,0:T(8,128)(2,1)S(1)} all-gather(bf16[128,768]{1,0:T(8,128)(2,1)} %reduce-scatter.5.cloned.1.call-done), channel_id=1, replica_groups=mesh['groups'=2,'loop'=4,'enc'=2,'rep'=2] {'enc'}, dimensions={0}, use_global_device_ids=true | all-gather | bytes 589824 | tf_op jit(solution)/shard_map/all_gather | solution.py:93
  99.5 1.4 convolution_bitcast_fusion
  100.9 0.0 all-reduce.2.cloned.1.call-update
  100.9 1.1 convolution_convert_fusion
  102.0 58.8 %all-reduce.2.cloned.1.call-done = f32[384,768]{0,1:T(8,128)} async-done(((f32[384,768]{0,1:T(8,128)}), f32[384,768]{0,1:T(8,128)}) %all-reduce.2.cloned.1.call-update) | async-done | bytes 1179664 | tf_op jit(solution)/shard_map/psum | solution.py:103
  160.8 2.7 %copy.9 = f32[384,768]{1,0:T(8,128)} copy(f32[384,768]{0,1:T(8,128)} %all-reduce.2.cloned.1.call-done) | data formatting | bytes 2359296
  (13 shorter events, 0.1 us)
Async XLA Ops:
  7.2 1.1 copy-start
  7.2 3.3 %copy-start.2 = (s32[4]{0:T(128)S(1)}, s32[4]{0:T(128)}, u32[]{:S(2)}) copy-start(s32[4]{0:T(128)} %param.9) | copy-start | bytes 52
  7.2 23.8 %reduce-scatter.3.cloned.1.call-start = ((), (), s32[]{:S(2)}) async-start(), calls=%async_computation.2 | async-start | bytes 1179648 | tf_op jit(solution)/shard_map/reduce_scatter | solution.py:30
  10.4 81.6 %reduce-scatter.5.cloned.1.call-start = ((), (), s32[]{:S(2)}) async-start(), calls=%async_computation.3 | async-start | bytes 983040 | tf_op jit(solution)/shard_map/reduce_scatter | solution.py:90
  41.5 9.0 %collective-permute-start = (bf16[128,768]{1,0:T(8,128)(2,1)S(1)}, bf16[128,768]{1,0:T(8,128)(2,1)S(1)}, u32[]{:S(2)}, u32[]{:S(2)}) collective-permute-start(bf16[128,768]{1,0:T(8,128)(2,1)S(1)} %get-tuple-element.558), channel_id=1, source_target_pairs={{0,4},{4,8},{8,12},{12,0},{1,5},{5,9},{9,13},{13,1},{2,6},{6,10},{... | collective-permute-start | bytes 589832 | tf_op jit(solution)/shard_map/while/body/eval_jaxpr/ppermute | solution.py:12
  51.7 8.2 %collective-permute-start = (bf16[128,768]{1,0:T(8,128)(2,1)S(1)}, bf16[128,768]{1,0:T(8,128)(2,1)S(1)}, u32[]{:S(2)}, u32[]{:S(2)}) collective-permute-start(bf16[128,768]{1,0:T(8,128)(2,1)S(1)} %get-tuple-element.558), channel_id=1, source_target_pairs={{0,4},{4,8},{8,12},{12,0},{1,5},{5,9},{9,13},{13,1},{2,6},{6,10},{... | collective-permute-start | bytes 589832 | tf_op jit(solution)/shard_map/while/body/eval_jaxpr/ppermute | solution.py:12
  61.1 7.5 %collective-permute-start = (bf16[128,768]{1,0:T(8,128)(2,1)S(1)}, bf16[128,768]{1,0:T(8,128)(2,1)S(1)}, u32[]{:S(2)}, u32[]{:S(2)}) collective-permute-start(bf16[128,768]{1,0:T(8,128)(2,1)S(1)} %get-tuple-element.558), channel_id=1, source_target_pairs={{0,4},{4,8},{8,12},{12,0},{1,5},{5,9},{9,13},{13,1},{2,6},{6,10},{... | collective-permute-start | bytes 589832 | tf_op jit(solution)/shard_map/while/body/eval_jaxpr/ppermute | solution.py:12
  69.8 29.7 %copy-start.1 = (bf16[256,384]{1,0:T(8,128)(2,1)S(1)}, bf16[256,384]{1,0:T(8,128)(2,1)}, u32[]{:S(2)}) copy-start(bf16[256,384]{1,0:T(8,128)(2,1)} %param.6) | copy-start | bytes 589828
  71.0 89.8 %all-reduce.2.cloned.1.call-start = ((), (), s32[]{:S(2)}) async-start(), calls=%async_computation.4 | async-start | bytes 2359296 | tf_op jit(solution)/shard_map/psum | solution.py:103
Sparse Core Ops, SparseCore 0:
  10.8 20.1 reduce-scatter.2
  71.1 20.8 reduce-scatter.4
  101.1 59.6 all-reduce.1
where the time goes:
time: 170 us
  waiting for transfers between devices  114 us (67%)
  blocking collectives  15.7 us (9%)
  between operations  13.8 us (8%)
  other arithmetic  9.37 us (6%)
  matrix products  8.66 us (5%)
  local copies, waits for them, and re-layouts  6.9 us (4%)
  starting transfers between devices  1.78 us (1%)
    psum x1, waiting for transfers between devices, body(): head_grad = lax.psum(head_part, ('loop', 'rep'))  58.8 us
    reduce_scatter x1, waiting for transfers between devices, body(): lax.psum_scatter(grad_block.astype(jnp.bfloat16), ('enc', 'rep'), scatter...  20.9 us
    ppermute x3, waiting for transfers between devices, passed_along(): return lax.ppermute(value, axis, pairs)  17 us
    reduce_scatter x1, waiting for transfers between devices, body(): lax.psum_scatter(jnp.dot(rows, head_weight, preferred_element_type=jnp.fl...  16.8 us
    all_gather x1, blocking collectives, body(): block_feats = lax.all_gather(own_feats, ('enc', 'rep'), axis=0, tiled=True)  8.2 us
    all_gather x1, blocking collectives, body(): piece = lax.all_gather(own_grad, 'enc', axis=0, tiled=True)  7.51 us
    select_n x4, other arithmetic, tile(): piece_coef = jnp.where(piece_offsets < anchor_count, piece_coef, 0.0)  5.68 us
    unnamed x7, local copies, waits for them, and re-layouts  3.67 us
  transfers between devices with their start and end apart: 6, of which 6 were waited for; matrix products, arithmetic and copies ran while one was open for 6% of the time, Pallas kernels for 0%

commit v1 on v0

--- a/solution.py
+++ b/solution.py
@@ -1,9 +1,13 @@
 import jax
 import jax.numpy as jnp
 from jax import lax
+from jax.experimental import pallas as pl
+from jax.experimental.pallas import tpu as pltpu
 from jax.sharding import PartitionSpec as P
 
 EPSILON = 1e-06
+TILE = 128
+CHUNK = 2 * TILE
 
 
 def passed_along(value, axis, steps):
@@ -12,11 +16,7 @@
     return lax.ppermute(value, axis, pairs)
 
 
-def pass_forward(piece):
-    return passed_along(piece, "loop", 1)
-
-
-def body(embeddings, head_weight, gp_weights, counts):
+def ring_body(embeddings, head_weight, gp_weights, counts):
     enc_size = lax.axis_size("enc")
     rep_size = lax.axis_size("rep")
     loop_size = lax.axis_size("loop")
@@ -26,9 +26,8 @@
     loop_index = lax.axis_index("loop")
     enc_index = lax.axis_index("enc")
     rep_index = lax.axis_index("rep")
-    rows = embeddings
     own_feats = lax.psum_scatter(
-        jnp.dot(rows, head_weight, preferred_element_type=jnp.float32),
+        jnp.dot(embeddings, head_weight, preferred_element_type=jnp.float32),
         "enc",
         scatter_dimension=0,
         tiled=True,
@@ -80,7 +79,7 @@
 
     def forward_step(step_index, carry):
         moving, inner = carry
-        moving = pass_forward(moving)
+        moving = passed_along(moving, "loop", 1)
         inner = tile(inner, moving, (loop_index - step_index - 1 + loop_size) % loop_size)
         return (moving, inner)
 
@@ -91,21 +90,234 @@
         grad_block.astype(jnp.bfloat16), ("enc", "rep"), scatter_dimension=0, tiled=True
     )
     piece = lax.all_gather(own_grad, "enc", axis=0, tiled=True)
-    back = lax.dot_general(
+    embed_part = lax.dot_general(
         piece, head_weight, (((1,), (1,)), ((), ())), preferred_element_type=jnp.float32
     )
-    embed_part = back
-    rows = embeddings
     head_part = lax.dot_general(
-        rows, piece, (((0,), (0,)), ((), ())), preferred_element_type=jnp.float32
-    )
-    embed_part, head_part = (embed_part, head_part)
+        embeddings, piece, (((0,), (0,)), ((), ())), preferred_element_type=jnp.float32
+    )
     head_grad = lax.psum(head_part, ("loop", "rep"))
     return (embed_part.astype(jnp.bfloat16), head_grad)
 
 
+OWN_ORDER = ((0, 0), (0, 1), (2, 0), (2, 1), (3, 1), (3, 0), (1, 1), (1, 0))
+SLOTS = [(0, k, h) for k, h in OWN_ORDER] + [(1, k, h) for k, h in OWN_ORDER[::-1]]
+LENT = ((1, 0), (1, 1), (3, 0), (3, 1))
+PLACES = 24
+
+
+def turned(row):
+    return jnp.transpose(jnp.broadcast_to(row, (TILE, TILE)))[:, :1]
+
+
+def prep_kernel(counts_ref, gp_ref, weights, places):
+    z = lax.axis_index("loop")
+    rep = lax.axis_index("rep")
+    lane = lax.broadcasted_iota(jnp.int32, (1, TILE), 1)
+    weights[...] = jnp.zeros_like(weights)
+    total = jnp.int32(0)
+    totals = []
+    for slot, (other, k, h) in enumerate(SLOTS):
+        block = jnp.bitwise_xor(z, k)
+        piece = rep if other == 0 else 1 - rep
+        base = piece * (2 * TILE) + h * TILE
+        count = counts_ref[block]
+        valid = count > base
+
+        @pl.when(valid)
+        def _(block=block, piece=piece, h=h, base=base, count=count, total=total):
+            row = gp_ref[pl.ds(block * 4 + piece * 2 + h, 1), :]
+            weights[pl.ds(total, 1), :] = jnp.where(lane + base < count, row, 0.0)
+
+        places[slot] = jnp.where(valid, total, -1)
+        total = total + valid.astype(jnp.int32)
+        totals.append(total)
+    own = totals[len(OWN_ORDER) - 1]
+    places[16] = total
+    places[17] = jnp.where(rep == 0, (total + 1) // 2, total // 2)
+    places[18] = jnp.clip(counts_ref[z] - rep * (2 * TILE), 0, 2 * TILE)
+    places[19] = own
+
+
+def pair_kernel(places, weights, head_ref, *refs):
+    near_refs, lent_refs = refs[:4], {1: refs[4], 3: refs[5]}
+    feat_refs = (refs[6:10], refs[10:14])
+    embed_out, head_out = refs[14:16]
+    near, feats, norms, grads = refs[16:]
+    width = head_ref.shape[1]
+    total, rows_here, own_valid = places[16], places[17], places[18]
+
+    def tile_at(place):
+        return pl.ds(pl.multiple_of(place * TILE, TILE), TILE)
+
+    for slot, (other, k, h) in enumerate(SLOTS):
+        place = places[slot]
+
+        @pl.when(place >= 0)
+        def _(place=place, other=other, k=k, h=h):
+            here = slice(h * TILE, (h + 1) * TILE)
+            value = feat_refs[other][k][here, :]
+            feats[tile_at(place), :] = value
+            wide = value.astype(jnp.float32)
+            square = wide * wide
+            part = square[:, :TILE]
+            for s in range(1, width // TILE):
+                part += square[:, s * TILE : (s + 1) * TILE]
+            norms[pl.ds(place, 1), :] = jnp.sum(jnp.transpose(part), axis=0, keepdims=True)
+            if other == 0:
+                near[tile_at(place), :] = near_refs[k][here, :]
+            elif (k, h) in LENT:
+                near[tile_at(place), :] = lent_refs[k][here, :]
+
+    feats[tile_at(total), :] = jnp.zeros((TILE, width), jnp.bfloat16)
+    norms[pl.ds(total, 1), :] = jnp.zeros((1, TILE), jnp.float32)
+
+    def row_chunk(i, tiles):
+        rows = pl.ds(pl.multiple_of(i * CHUNK, CHUNK), CHUNK)
+        left = feats[rows, :]
+        right = feats[: tiles * TILE, :]
+        pair_of = [pl.ds(2 * i, 1), pl.ds(2 * i + 1, 1)]
+        left_norms = jnp.concatenate([turned(norms[at, :]) for at in pair_of], axis=0)
+        coef = jnp.concatenate([turned(weights[at, :]) for at in pair_of], axis=0)
+        scores = lax.dot_general(
+            left, right, (((1,), (1,)), ((), ())), preferred_element_type=jnp.float32
+        )
+        all_norms = jnp.concatenate([norms[t : t + 1, :] for t in range(tiles)], axis=1)
+        all_coef = jnp.concatenate([weights[t : t + 1, :] for t in range(tiles)], axis=1)
+        both = left_norms + all_norms
+        denom = both - scores + EPSILON
+        scaled = all_coef * (1.0 / (denom * denom))
+        pair = (scaled * both).astype(jnp.bfloat16)
+        quotient = 2.0 * jnp.sum(scaled * scores, axis=1, keepdims=True)
+        carried = jnp.dot(pair, right, preferred_element_type=jnp.float32)
+        row = lax.broadcasted_iota(jnp.int32, (CHUNK, 1), 0) + i * CHUNK
+        coef = jnp.where(row < rows_here * TILE, coef, 0.0)
+        grad = coef * (carried - left.astype(jnp.float32) * quotient)
+        grads[rows, :] = grad.astype(jnp.bfloat16)
+
+    chunks = (rows_here + 1) // 2
+    behind = 2 * chunks - 1
+
+    @pl.when(behind >= rows_here)
+    def _():
+        near[tile_at(behind), :] = jnp.zeros((TILE, near.shape[1]), near.dtype)
+
+    col_tiles = jnp.maximum(2 * ((total + 1) // 2), 8)
+    for tiles in (8, 10, 12, 14):
+
+        @pl.when(col_tiles == tiles)
+        def _(tiles=tiles):
+            def step(i, _):
+                row_chunk(i, tiles)
+                return 0
+
+            lax.fori_loop(0, chunks, step, 0)
+
+    for count in (1, 2, 3, 4):
+
+        @pl.when(chunks == count)
+        def _(count=count):
+            rows = slice(0, count * CHUNK)
+            head_out[...] = lax.dot_general(
+                near[rows, :],
+                grads[rows, :],
+                (((0,), (0,)), ((), ())),
+                preferred_element_type=jnp.float32,
+            )
+
+    own = grads[:CHUNK, :]
+    row = lax.broadcasted_iota(jnp.int32, (CHUNK, 1), 0)
+    own = jnp.where(row < own_valid, own, jnp.zeros_like(own))
+    embed_out[...] = lax.dot_general(
+        own, head_ref[...], (((1,), (1,)), ((), ())), preferred_element_type=jnp.float32
+    ).astype(embed_out.dtype)
+
+
+def gathered_body(embeddings, head_weight, gp_weights, counts):
+    loop_size = lax.axis_size("loop")
+    rep = lax.axis_index("rep")
+    share_rows, share_cols = embeddings.shape
+    enc_rows, width = head_weight.shape
+
+    def across_z(value, step):
+        return lax.ppermute(value, "loop", [(i, i ^ step) for i in range(loop_size)])
+
+    def across_x(value):
+        return lax.ppermute(value, "enc", [(0, 1), (1, 0)])
+
+    def across_cores(value):
+        return lax.ppermute(value, "rep", [(0, 1), (1, 0)])
+
+    smem = pl.BlockSpec(memory_space=pltpu.SMEM)
+    vmem = pl.BlockSpec(memory_space=pltpu.VMEM)
+    weights, places = pl.pallas_call(
+        prep_kernel,
+        out_shape=(
+            jax.ShapeDtypeStruct((PLACES, TILE), jnp.float32),
+            jax.ShapeDtypeStruct((PLACES,), jnp.int32),
+        ),
+        in_specs=[smem, vmem],
+        out_specs=(vmem, smem),
+    )(counts, gp_weights.reshape(-1, TILE))
+
+    far0 = across_x(embeddings)
+    near3 = across_z(embeddings, 3)
+    near1 = across_z(embeddings, 1)
+    half = enc_rows // 2
+    head_mine = across_x(lax.dynamic_slice_in_dim(head_weight, rep * half, half, 0))
+    head_other = across_cores(head_mine)
+    far_head = jnp.where(
+        rep == 0,
+        jnp.concatenate([head_mine, head_other]),
+        jnp.concatenate([head_other, head_mine]),
+    )
+    near2 = across_z(near3, 1)
+    far2 = across_z(far0, 2)
+    far1 = across_x(near1)
+    far3 = across_x(near3)
+    near = [embeddings, near1, near2, near3]
+    far = [far0, far1, far2, far3]
+    feats = [
+        (
+            jnp.dot(a, head_weight, preferred_element_type=jnp.float32)
+            + jnp.dot(b, far_head, preferred_element_type=jnp.float32)
+        ).astype(jnp.bfloat16)
+        for a, b in zip(near, far)
+    ]
+    feats_other = [across_cores(value) for value in feats]
+    lent = [across_cores(near1), across_cores(near3)]
+
+    embed_grad, head_part = pl.pallas_call(
+        pair_kernel,
+        out_shape=(
+            jax.ShapeDtypeStruct((share_rows, share_cols), jnp.bfloat16),
+            jax.ShapeDtypeStruct((enc_rows, width), jnp.float32),
+        ),
+        in_specs=[smem] + [vmem] * 16,
+        out_specs=(vmem, vmem),
+        scratch_shapes=[
+            pltpu.VMEM((12 * TILE, share_cols), jnp.bfloat16),
+            pltpu.VMEM((18 * TILE, width), jnp.bfloat16),
+            pltpu.VMEM((PLACES, TILE), jnp.float32),
+            pltpu.VMEM((4 * CHUNK, width), jnp.bfloat16),
+        ],
+        compiler_params=pltpu.CompilerParams(vmem_limit_bytes=40 * 2**20),
+    )(places, weights, head_weight, *near, *lent, *feats, *feats_other)
+    head_grad = head_part + across_cores(head_part)
+    return embed_grad, head_grad
+
+
 def solution(mesh):
     placed = (P(("groups", "loop", "rep"), "enc"), P("enc", None), P("groups"), P("groups"))
+    sizes = dict(mesh.shape)
+
+    def body(*arrays):
+        share_rows = arrays[0].shape[0]
+        small = sizes["loop"] == 4 and sizes["enc"] == 2 and sizes["rep"] == 2
+        if small and share_rows == 2 * TILE:
+            return gathered_body(*arrays)
+        return ring_body(*arrays)
+
     return jax.shard_map(
         body,
         mesh=mesh,

time: 170 us -> 55 us (0.32)
  waiting for transfers between devices: 114 us -> 22.2 us
  blocking collectives: 15.7 us -> 0 us
  between operations: 13.8 us -> 0.77 us
  starting transfers between devices: 1.78 us -> 13.4 us
  Pallas kernels: 0 us -> 9.94 us
  other arithmetic: 9.37 us -> 1.17 us
  local copies, waits for them, and re-layouts: 6.9 us -> 2.36 us
  matrix products: 8.66 us -> 4.86 us
    psum x1 -> x0, waiting for transfers between devices: 58.8 us -> none  [body(): head_grad = lax.psum(head_part, ('loop', 'rep'))]
    reduce_scatter x2 -> x0, waiting for transfers between devices: 37.7 us -> none  [the longest x1 20.9 us: body(): lax.psum_scatter(grad_block.astype(jnp.bfloat16), ('enc', 'rep'), scatter...]
    all_gather x2 -> x0, blocking collectives: 15.7 us -> none  [the longest x1 8.2 us: body(): block_feats = lax.all_gather(own_feats, ('enc', 'rep'), axis=0, tiled=True)]
    ppermute x3 -> x16, starting transfers between devices: 1.66 us -> 13.4 us  [the longest x4 6.36 us: across_z(): lax.ppermute(value, 'loop', [(i, i ^ step) for i in range(loop_size)])]
    pallas_call x0 -> x2, Pallas kernels: none -> 9.94 us  [the longest x1 8.47 us: gathered_body(): pl.pallas_call(pair_kernel, out_shape=(jax.ShapeDtypeStruct((share_rows,...]
    select_n x5 -> x0, other arithmetic: 6.43 us -> none  [the longest x4 5.68 us: tile(): piece_coef = jnp.where(piece_offsets < anchor_count, piece_coef, 0.0)]
    ppermute x3 -> x16, waiting for transfers between devices: 17 us -> 22.2 us  [the longest x4 15.7 us: across_z(): lax.ppermute(value, 'loop', [(i, i ^ step) for i in range(loop_size)])]
    dot_general x11 -> x8, matrix products: 8.66 us -> 4.86 us  [the longest x4 2.61 us: gathered_body(): jnp.dot(a, head_weight, preferred_element_type=jnp.float32)]
  transfers between devices with their start and end apart: 6 -> 16, of which waited for: 6 -> 7; matrix products, arithmetic and copies ran while one was open for 6% -> 9% of each run, Pallas kernels for 0% -> 3%
where the time goes in v1:
time: 55 us; the launch traced here: 54.7 us
  waiting for transfers between devices  22.2 us (40%)
  starting transfers between devices  13.4 us (24%)
  Pallas kernels  9.94 us (18%)
  matrix products  4.86 us (9%)
  local copies, waits for them, and re-layouts  2.36 us (4%)
  other arithmetic  1.17 us (2%)
  between operations  0.77 us (1%)
    ppermute x4, waiting for transfers between devices, across_z(): lax.ppermute(value, 'loop', [(i, i ^ step) for i in range(loop_size)])  15.7 us
    pallas_call x1, Pallas kernels, gathered_body(): pl.pallas_call(pair_kernel, out_shape=(jax.ShapeDtypeStruct((share_rows,...  8.47 us
    ppermute x4, starting transfers between devices, across_z(): lax.ppermute(value, 'loop', [(i, i ^ step) for i in range(loop_size)])  6.36 us
    ppermute x4, starting transfers between devices, across_x(): return lax.ppermute(value, 'enc', [(0, 1), (1, 0)])  5.31 us
    ppermute x4, waiting for transfers between devices, across_x(): return lax.ppermute(value, 'enc', [(0, 1), (1, 0)])  3.32 us
    ppermute x8, waiting for transfers between devices, across_cores(): return lax.ppermute(value, 'rep', [(0, 1), (1, 0)])  3.19 us
    dot_general x4, matrix products, gathered_body(): jnp.dot(a, head_weight, preferred_element_type=jnp.float32)  2.61 us
    dot_general x4, matrix products, gathered_body(): jnp.dot(b, far_head, preferred_element_type=jnp.float32)  2.25 us
  transfers between devices with their start and end apart: 16, of which 7 were waited for; matrix products, arithmetic and copies ran while one was open for 9% of the time, Pallas kernels for 3%

profile of v1, /device:TPU:0, one launch (start us, length us, event | category | flops | bytes accessed | tf_op | source)
XLA Modules:
  0.0 54.7 jit_solution(16691792998516314276)
XLA Ops:
  0.6 0.0 copy-start
  0.6 1.0 %constant_dynamic-slice_fusion = bf16[192,768]{1,0:T(8,128)(2,1)S(1)} fusion(bf16[384,768]{1,0:T(8,128)(2,1)} %head_ref.1, s32[]{:T(128)S(6)} %select_n.12), kind=kLoop, calls=%fused_computation.13 | loop fusion | bytes 589828 | tf_op jit(solution)/shard_map/dynamic_slice | solution.py:267
  1.7 3.0 %collective-permute-start.5 = (bf16[192,768]{1,0:T(8,128)(2,1)S(1)}, bf16[192,768]{1,0:T(8,128)(2,1)S(1)}, u32[]{:S(2)}, u32[]{:S(2)}) collective-permute-start(bf16[192,768]{1,0:T(8,128)(2,1)S(1)} %constant_dynamic-slice_fusion), channel_id=1, source_target_pairs={{0,2},{2,0},{1,3},{3,1},{4,6},{6,4},{5,7},{7,5},{8,10},{10,8},{9,1... | collective-permute-start | bytes 884744 | tf_op jit(solution)/shard_map/ppermute | solution.py:246
  4.7 3.6 %collective-permute-start.1 = (bf16[256,384]{1,0:T(8,128)(2,1)}, bf16[256,384]{1,0:T(8,128)(2,1)S(1)}, u32[]{:S(2)}, u32[]{:S(2)}) collective-permute-start(bf16[256,384]{1,0:T(8,128)(2,1)} %refs_0_.1), channel_id=1, source_target_pairs={{0,12},{4,8},{8,4},{12,0},{1,13},{5,9},{9,5},{13,1},{2,14},{6,10},... | collective-permute-start | bytes 589832 | tf_op jit(solution)/shard_map/ppermute | solution.py:243
  8.3 0.0 collective-permute-start
  8.3 0.5 collective-permute-start.7
  8.8 1.5 %fusion.7 = f32[256,768]{1,0:T(8,128)S(1)} fusion(bf16[256,384]{1,0:T(8,128)(2,1)} %refs_0_.1, bf16[384,768]{1,0:T(8,128)(2,1)} %head_ref.1), kind=kOutput, calls=%fused_computation.14 | convolution fusion | flops 150994944 | bytes 1572864 | tf_op jit(solution)/shard_map/dot_general | solution.py:282
  10.4 4.2 %collective-permute-done.1.refs_3_ = bf16[256,384]{1,0:T(8,128)(2,1)S(1)} collective-permute-done((bf16[256,384]{1,0:T(8,128)(2,1)}, bf16[256,384]{1,0:T(8,128)(2,1)S(1)}, u32[]{:S(2)}, u32[]{:S(2)}) %collective-permute-start.1) | collective-permute-done | bytes 196640 | tf_op jit(solution)/shard_map/ppermute | solution.py:243
  14.5 0.3 collective-permute-start.10
  14.8 0.0 collective-permute-start.4
  14.8 0.0 collective-permute-done.5
  14.8 0.5 collective-permute-start.6
  15.3 0.4 fusion.9
  15.7 1.7 %collective-permute-done.refs_1_ = bf16[256,384]{1,0:T(8,128)(2,1)S(1)} collective-permute-done((bf16[256,384]{1,0:T(8,128)(2,1)}, bf16[256,384]{1,0:T(8,128)(2,1)S(1)}, u32[]{:S(2)}, u32[]{:S(2)}) %collective-permute-start) | collective-permute-done | bytes 196640 | tf_op jit(solution)/shard_map/ppermute | solution.py:243
  17.4 1.7 %collective-permute-start.2 = (bf16[256,384]{1,0:T(8,128)(2,1)S(1)}, bf16[256,384]{1,0:T(8,128)(2,1)S(1)}, u32[]{:S(2)}, u32[]{:S(2)}) collective-permute-start(bf16[256,384]{1,0:T(8,128)(2,1)S(1)} %collective-permute-done.1.refs_3_), channel_id=1, source_target_pairs={{0,4},{4,0},{8,12},{12,8},{1,5},{5,1},{9,13},{13,9},{2,6},{6,2},{1... | collective-permute-start | bytes 589832 | tf_op jit(solution)/shard_map/ppermute | solution.py:243
  19.1 0.0 collective-permute-done.7
  19.1 1.1 %collective-permute-start.9 = (bf16[256,384]{1,0:T(8,128)(2,1)S(1)}, bf16[256,384]{1,0:T(8,128)(2,1)S(1)}, u32[]{:S(2)}, u32[]{:S(2)}) collective-permute-start(bf16[256,384]{1,0:T(8,128)(2,1)S(1)} %collective-permute-done.7), channel_id=1, source_target_pairs={{0,8},{4,12},{8,0},{12,4},{1,9},{5,13},{9,1},{13,5},{2,10},{6,14},... | collective-permute-start | bytes 589832 | tf_op jit(solution)/shard_map/ppermute | solution.py:243
  20.2 0.4 fusion.8
  20.6 9.7 %collective-permute-done.9 = bf16[256,384]{1,0:T(8,128)(2,1)S(1)} collective-permute-done((bf16[256,384]{1,0:T(8,128)(2,1)S(1)}, bf16[256,384]{1,0:T(8,128)(2,1)S(1)}, u32[]{:S(2)}, u32[]{:S(2)}) %collective-permute-start.9) | collective-permute-done | bytes 196640 | tf_op jit(solution)/shard_map/ppermute | solution.py:243
  30.3 1.5 %collective-permute-start.8 = (bf16[256,384]{1,0:T(8,128)(2,1)S(1)}, bf16[256,384]{1,0:T(8,128)(2,1)S(1)}, u32[]{:S(2)}, u32[]{:S(2)}) collective-permute-start(bf16[256,384]{1,0:T(8,128)(2,1)S(1)} %collective-permute-done.refs_1_), channel_id=1, source_target_pairs={{0,2},{2,0},{1,3},{3,1},{4,6},{6,4},{5,7},{7,5},{8,10},{10,8},{9,1... | collective-permute-start | bytes 589832 | tf_op jit(solution)/shard_map/ppermute | solution.py:246
  31.8 0.0 collective-permute-done.6
  31.8 0.4 convolution_bitcast_fusion.1
  32.2 0.0 copy-start.5
  32.2 0.0 collective-permute-done.2.refs_2_
  32.2 0.4 fusion.6.refs_8_
  32.6 0.1 collective-permute-start.13
  32.7 3.3 %collective-permute-done.8 = bf16[256,384]{1,0:T(8,128)(2,1)S(1)} collective-permute-done((bf16[256,384]{1,0:T(8,128)(2,1)S(1)}, bf16[256,384]{1,0:T(8,128)(2,1)S(1)}, u32[]{:S(2)}, u32[]{:S(2)}) %collective-permute-start.8) | collective-permute-done | bytes 196640 | tf_op jit(solution)/shard_map/ppermute | solution.py:246
  36.0 0.4 fusion.4.refs_7_
  36.4 0.0 copy-start.7
  36.4 0.1 collective-permute-start.12
  36.5 0.0 collective-permute-done.10
  36.5 0.4 fusion.5.refs_9_
  36.9 0.0 copy-start.1
  36.9 0.6 %collective-permute-start.14 = (bf16[256,768]{1,0:T(8,128)(2,1)S(1)}, bf16[256,768]{1,0:T(8,128)(2,1)}, u32[]{:S(2)}, u32[]{:S(2)}) collective-permute-start(bf16[256,768]{1,0:T(8,128)(2,1)S(1)} %fusion.5.refs_9_), channel_id=1, source_target_pairs={{0,1},{1,0},{2,3},{3,2},{4,5},{5,4},{6,7},{7,6},{8,9},{9,8},{10,11... | collective-permute-start | bytes 1179656 | tf_op jit(solution)/shard_map/ppermute | solution.py:249
  37.4 1.1 %fusion.3.refs_6_ = bf16[256,768]{1,0:T(8,128)(2,1)} fusion(f32[256,768]{1,0:T(8,128)S(1)} %fusion.7, bf16[256,384]{1,0:T(8,128)(2,1)S(1)} %copy-done.7, bf16[192,768]{1,0:T(8,128)(2,1)S(1)} %collective-permute-done.6, bf16[192,768]{1,0:T(8,128)(2,1)S(1)} %copy-done.5, pred[]{:T(512)S(6)} %eq.3), kind=kOutput, calls=%fused_computation.8 | convolution fusion | flops 154042368 | bytes 1966081 | tf_op jit(solution)/shard_map/dot_general | solution.py:283
  38.5 0.0 collective-permute-start.11
  38.6 0.0 collective-permute-done.4.refs_5_
  38.6 0.5 collective-permute-start.3
  39.1 1.5 %shard_map.59 = (f32[24,128]{1,0:T(8,128)}, s32[24]{0:T(128)}) custom-call(s32[4]{0:T(128)} %counts_ref.1, f32[16,128]{1,0:T(8,128)} %bitcast.33), custom_call_target="tpu_custom_call" | custom-call | tf_op jit(solution)/shard_map/pallas_call | solution.py:253
  40.5 0.1 collective-permute-done.3.refs_4_
  40.7 0.0 collective-permute-done.13.refs_12_
  40.7 0.0 collective-permute-done.12.refs_11_
  40.7 0.2 collective-permute-done.11.refs_10_
  40.9 0.7 %copy-done.2 = f32[24,128]{1,0:T(8,128)S(1)} copy-done((f32[24,128]{1,0:T(8,128)S(1)}, f32[24,128]{1,0:T(8,128)}, u32[]{:S(2)}) %copy-start.2) | copy-done | bytes 12312
  41.6 0.6 %copy-done.3 = s32[24]{0:T(128)S(1)} copy-done((s32[24]{0:T(128)S(1)}, s32[24]{0:T(128)}, u32[]{:S(2)}) %copy-start.3) | copy-done | bytes 120
  42.2 8.5 %shard_map.60 = (bf16[256,384]{1,0:T(8,128)(2,1)}, f32[384,768]{1,0:T(8,128)S(1)}) custom-call(s32[24]{0:T(128)S(1)} %copy-done.3, f32[24,128]{1,0:T(8,128)S(1)} %copy-done.2, bf16[384,768]{1,0:T(8,128)(2,1)S(1)} %copy-done, bf16[256,384]{1,0:T(8,128)(2,1)S(1)} %copy-done.1, bf16[256,384]{1,0:T(8,128)(2,1)S(1)} %collective-permute-done.refs_1_, ...), custom_call_target="tpu_custom_call" | custom-call | tf_op jit(solution)/shard_map/pallas_call | solution.py:290
  50.6 2.8 %collective-permute-done.15 = f32[384,768]{1,0:T(8,128)S(1)} collective-permute-done((f32[384,768]{1,0:T(8,128)S(1)}, f32[384,768]{1,0:T(8,128)S(1)}, u32[]{:S(2)}, u32[]{:S(2)}) %collective-permute-start.15) | collective-permute-done | bytes 1179680 | tf_op jit(solution)/shard_map/ppermute | solution.py:249
  53.5 1.2 %add.23 = f32[384,768]{1,0:T(8,128)} add(f32[384,768]{1,0:T(8,128)S(1)} %get-tuple-element.9, f32[384,768]{1,0:T(8,128)S(1)} %collective-permute-done.15) | non-fusion elementwise | flops 294912 | bytes 3538944 | tf_op jit(solution)/shard_map/add | solution.py:306
  (12 shorter events, 0.0 us)
Async XLA Ops:
  0.6 14.7 %copy-start = (bf16[384,768]{1,0:T(8,128)(2,1)S(1)}, bf16[384,768]{1,0:T(8,128)(2,1)}, u32[]{:S(2)}) copy-start(bf16[384,768]{1,0:T(8,128)(2,1)} %head_ref.1) | copy-start | bytes 1769476
  1.7 13.1 %collective-permute-start.5 = (bf16[192,768]{1,0:T(8,128)(2,1)S(1)}, bf16[192,768]{1,0:T(8,128)(2,1)S(1)}, u32[]{:S(2)}, u32[]{:S(2)}) collective-permute-start(bf16[192,768]{1,0:T(8,128)(2,1)S(1)} %constant_dynamic-slice_fusion), channel_id=1, source_target_pairs={{0,2},{2,0},{1,3},{3,1},{4,6},{6,4},{5,7},{7,5},{8,10},{10,8},{9,1... | collective-permute-start | bytes 884744 | tf_op jit(solution)/shard_map/ppermute | solution.py:246
  4.7 9.8 %collective-permute-start.1 = (bf16[256,384]{1,0:T(8,128)(2,1)}, bf16[256,384]{1,0:T(8,128)(2,1)S(1)}, u32[]{:S(2)}, u32[]{:S(2)}) collective-permute-start(bf16[256,384]{1,0:T(8,128)(2,1)} %refs_0_.1), channel_id=1, source_target_pairs={{0,12},{4,8},{8,4},{12,0},{1,13},{5,9},{9,5},{13,1},{2,14},{6,10},... | collective-permute-start | bytes 589832 | tf_op jit(solution)/shard_map/ppermute | solution.py:243
  8.3 9.1 %collective-permute-start = (bf16[256,384]{1,0:T(8,128)(2,1)}, bf16[256,384]{1,0:T(8,128)(2,1)S(1)}, u32[]{:S(2)}, u32[]{:S(2)}) collective-permute-start(bf16[256,384]{1,0:T(8,128)(2,1)} %refs_0_.1), channel_id=1, source_target_pairs={{0,4},{4,0},{8,12},{12,8},{1,5},{5,1},{9,13},{13,9},{2,6},{6,2},{1... | collective-permute-start | bytes 589832 | tf_op jit(solution)/shard_map/ppermute | solution.py:243
  8.3 10.8 %collective-permute-start.7 = (bf16[256,384]{1,0:T(8,128)(2,1)}, bf16[256,384]{1,0:T(8,128)(2,1)S(1)}, u32[]{:S(2)}, u32[]{:S(2)}) collective-permute-start(bf16[256,384]{1,0:T(8,128)(2,1)} %refs_0_.1), channel_id=1, source_target_pairs={{0,2},{2,0},{1,3},{3,1},{4,6},{6,4},{5,7},{7,5},{8,10},{10,8},{9,1... | collective-permute-start | bytes 589832 | tf_op jit(solution)/shard_map/ppermute | solution.py:246
  14.5 21.9 %collective-permute-start.10 = (bf16[256,384]{1,0:T(8,128)(2,1)S(1)}, bf16[256,384]{1,0:T(8,128)(2,1)S(1)}, u32[]{:S(2)}, u32[]{:S(2)}) collective-permute-start(bf16[256,384]{1,0:T(8,128)(2,1)S(1)} %collective-permute-done.1.refs_3_), channel_id=1, source_target_pairs={{0,2},{2,0},{1,3},{3,1},{4,6},{6,4},{5,7},{7,5},{8,10},{10,8},{9,1... | collective-permute-start | bytes 589832 | tf_op jit(solution)/shard_map/ppermute | solution.py:246
  14.8 23.8 %collective-permute-start.4 = (bf16[256,384]{1,0:T(8,128)(2,1)S(1)}, bf16[256,384]{1,0:T(8,128)(2,1)S(1)}, u32[]{:S(2)}, u32[]{:S(2)}) collective-permute-start(bf16[256,384]{1,0:T(8,128)(2,1)S(1)} %collective-permute-done.1.refs_3_), channel_id=1, source_target_pairs={{0,1},{1,0},{2,3},{3,2},{4,5},{5,4},{6,7},{7,6},{8,9},{9,8},{10,11... | collective-permute-start | bytes 589832 | tf_op jit(solution)/shard_map/ppermute | solution.py:249
  14.8 17.0 %copy-start.4 = (bf16[192,768]{1,0:T(8,128)(2,1)}, bf16[192,768]{1,0:T(8,128)(2,1)S(1)}, u32[]{:S(2)}) copy-start(bf16[192,768]{1,0:T(8,128)(2,1)S(1)} %collective-permute-done.5) | copy-start | bytes 884740
  14.8 17.0 %collective-permute-start.6 = (bf16[192,768]{1,0:T(8,128)(2,1)S(1)}, bf16[192,768]{1,0:T(8,128)(2,1)S(1)}, u32[]{:S(2)}, u32[]{:S(2)}) collective-permute-start(bf16[192,768]{1,0:T(8,128)(2,1)S(1)} %collective-permute-done.5), channel_id=1, source_target_pairs={{0,1},{1,0},{2,3},{3,2},{4,5},{5,4},{6,7},{7,6},{8,9},{9,8},{10,11... | collective-permute-start | bytes 884744 | tf_op jit(solution)/shard_map/ppermute | solution.py:249
  17.4 14.8 %collective-permute-start.2 = (bf16[256,384]{1,0:T(8,128)(2,1)S(1)}, bf16[256,384]{1,0:T(8,128)(2,1)S(1)}, u32[]{:S(2)}, u32[]{:S(2)}) collective-permute-start(bf16[256,384]{1,0:T(8,128)(2,1)S(1)} %collective-permute-done.1.refs_3_), channel_id=1, source_target_pairs={{0,4},{4,0},{8,12},{12,8},{1,5},{5,1},{9,13},{13,9},{2,6},{6,2},{1... | collective-permute-start | bytes 589832 | tf_op jit(solution)/shard_map/ppermute | solution.py:243
  19.1 12.7 %copy-start.6 = (bf16[256,384]{1,0:T(8,128)(2,1)}, bf16[256,384]{1,0:T(8,128)(2,1)S(1)}, u32[]{:S(2)}) copy-start(bf16[256,384]{1,0:T(8,128)(2,1)S(1)} %collective-permute-done.7) | copy-start | bytes 589828
  19.1 11.2 %collective-permute-start.9 = (bf16[256,384]{1,0:T(8,128)(2,1)S(1)}, bf16[256,384]{1,0:T(8,128)(2,1)S(1)}, u32[]{:S(2)}, u32[]{:S(2)}) collective-permute-start(bf16[256,384]{1,0:T(8,128)(2,1)S(1)} %collective-permute-done.7), channel_id=1, source_target_pairs={{0,8},{4,12},{8,0},{12,4},{1,9},{5,13},{9,1},{13,5},{2,10},{6,14},... | collective-permute-start | bytes 589832 | tf_op jit(solution)/shard_map/ppermute | solution.py:243
  30.3 5.7 %collective-permute-start.8 = (bf16[256,384]{1,0:T(8,128)(2,1)S(1)}, bf16[256,384]{1,0:T(8,128)(2,1)S(1)}, u32[]{:S(2)}, u32[]{:S(2)}) collective-permute-start(bf16[256,384]{1,0:T(8,128)(2,1)S(1)} %collective-permute-done.refs_1_), channel_id=1, source_target_pairs={{0,2},{2,0},{1,3},{3,1},{4,6},{6,4},{5,7},{7,5},{8,10},{10,8},{9,1... | collective-permute-start | bytes 589832 | tf_op jit(solution)/shard_map/ppermute | solution.py:246
  32.2 3.8 %copy-start.5 = (bf16[192,768]{1,0:T(8,128)(2,1)S(1)}, bf16[192,768]{1,0:T(8,128)(2,1)}, u32[]{:S(2)}) copy-start(bf16[192,768]{1,0:T(8,128)(2,1)} %copy-done.4) | copy-start | bytes 884740
  32.6 8.1 %collective-permute-start.13 = (bf16[256,768]{1,0:T(8,128)(2,1)S(1)}, bf16[256,768]{1,0:T(8,128)(2,1)S(1)}, u32[]{:S(2)}, u32[]{:S(2)}) collective-permute-start(bf16[256,768]{1,0:T(8,128)(2,1)S(1)} %fusion.6.refs_8_), channel_id=1, source_target_pairs={{0,1},{1,0},{2,3},{3,2},{4,5},{5,4},{6,7},{7,6},{8,9},{9,8},{10,11... | collective-permute-start | bytes 1179656 | tf_op jit(solution)/shard_map/ppermute | solution.py:249
  36.4 1.0 %copy-start.7 = (bf16[256,384]{1,0:T(8,128)(2,1)S(1)}, bf16[256,384]{1,0:T(8,128)(2,1)}, u32[]{:S(2)}) copy-start(bf16[256,384]{1,0:T(8,128)(2,1)} %copy-done.6) | copy-start | bytes 589828
  36.4 4.3 %collective-permute-start.12 = (bf16[256,768]{1,0:T(8,128)(2,1)S(1)}, bf16[256,768]{1,0:T(8,128)(2,1)S(1)}, u32[]{:S(2)}, u32[]{:S(2)}) collective-permute-start(bf16[256,768]{1,0:T(8,128)(2,1)S(1)} %fusion.4.refs_7_), channel_id=1, source_target_pairs={{0,1},{1,0},{2,3},{3,2},{4,5},{5,4},{6,7},{7,6},{8,9},{9,8},{10,11... | collective-permute-start | bytes 1179656 | tf_op jit(solution)/shard_map/ppermute | solution.py:249
  36.9 4.0 %copy-start.1 = (bf16[256,384]{1,0:T(8,128)(2,1)S(1)}, bf16[256,384]{1,0:T(8,128)(2,1)}, u32[]{:S(2)}) copy-start(bf16[256,384]{1,0:T(8,128)(2,1)} %refs_0_.1) | copy-start | bytes 589828
  36.9 3.8 %collective-permute-start.14 = (bf16[256,768]{1,0:T(8,128)(2,1)S(1)}, bf16[256,768]{1,0:T(8,128)(2,1)}, u32[]{:S(2)}, u32[]{:S(2)}) collective-permute-start(bf16[256,768]{1,0:T(8,128)(2,1)S(1)} %fusion.5.refs_9_), channel_id=1, source_target_pairs={{0,1},{1,0},{2,3},{3,2},{4,5},{5,4},{6,7},{7,6},{8,9},{9,8},{10,11... | collective-permute-start | bytes 1179656 | tf_op jit(solution)/shard_map/ppermute | solution.py:249
  38.5 2.3 %collective-permute-start.11 = (bf16[256,768]{1,0:T(8,128)(2,1)}, bf16[256,768]{1,0:T(8,128)(2,1)}, u32[]{:S(2)}, u32[]{:S(2)}) collective-permute-start(bf16[256,768]{1,0:T(8,128)(2,1)} %fusion.3.refs_6_), channel_id=1, source_target_pairs={{0,1},{1,0},{2,3},{3,2},{4,5},{5,4},{6,7},{7,6},{8,9},{9,8},{10,11... | collective-permute-start | bytes 1179656 | tf_op jit(solution)/shard_map/ppermute | solution.py:249
  38.6 2.1 %collective-permute-start.3 = (bf16[256,384]{1,0:T(8,128)(2,1)S(1)}, bf16[256,384]{1,0:T(8,128)(2,1)}, u32[]{:S(2)}, u32[]{:S(2)}) collective-permute-start(bf16[256,384]{1,0:T(8,128)(2,1)S(1)} %collective-permute-done.refs_1_), channel_id=1, source_target_pairs={{0,1},{1,0},{2,3},{3,2},{4,5},{5,4},{6,7},{7,6},{8,9},{9,8},{10,11... | collective-permute-start | bytes 589832 | tf_op jit(solution)/shard_map/ppermute | solution.py:249
  40.9 0.7 %copy-start.2 = (f32[24,128]{1,0:T(8,128)S(1)}, f32[24,128]{1,0:T(8,128)}, u32[]{:S(2)}) copy-start(f32[24,128]{1,0:T(8,128)} %get-tuple-element.7.weights) | copy-start | bytes 36868
  41.6 0.6 %copy-start.3 = (s32[24]{0:T(128)S(1)}, s32[24]{0:T(128)}, u32[]{:S(2)}) copy-start(s32[24]{0:T(128)} %get-tuple-element.6.places) | copy-start | bytes 292
  50.6 2.8 %collective-permute-start.15 = (f32[384,768]{1,0:T(8,128)S(1)}, f32[384,768]{1,0:T(8,128)S(1)}, u32[]{:S(2)}, u32[]{:S(2)}) collective-permute-start(f32[384,768]{1,0:T(8,128)S(1)} %get-tuple-element.9), channel_id=1, source_target_pairs={{0,1},{1,0},{2,3},{3,2},{4,5},{5,4},{6,7},{7,6},{8,9},{9,8},{10,11... | collective-permute-start | bytes 3538952 | tf_op jit(solution)/shard_map/ppermute | solution.py:249

commit v2 on v1

--- a/solution.py
+++ b/solution.py
@@ -139,24 +139,21 @@
     places[19] = own
 
 
-def pair_kernel(places, weights, head_ref, *refs):
-    near_refs, lent_refs = refs[:4], {1: refs[4], 3: refs[5]}
-    feat_refs = (refs[6:10], refs[10:14])
-    embed_out, head_out = refs[14:16]
-    near, feats, norms, grads = refs[16:]
-    width = head_ref.shape[1]
-    total, rows_here, own_valid = places[16], places[17], places[18]
-
-    def tile_at(place):
-        return pl.ds(pl.multiple_of(place * TILE, TILE), TILE)
-
+def tile_at(place):
+    return pl.ds(pl.multiple_of(place * TILE, TILE), TILE)
+
+
+def pack_tiles(distances, places, own_feats, other_feats, own_near, lent, feats, norms, near):
+    width = feats.shape[1]
     for slot, (other, k, h) in enumerate(SLOTS):
+        if k not in distances:
+            continue
         place = places[slot]
 
         @pl.when(place >= 0)
         def _(place=place, other=other, k=k, h=h):
             here = slice(h * TILE, (h + 1) * TILE)
-            value = feat_refs[other][k][here, :]
+            value = (other_feats if other else own_feats)[k][here, :]
             feats[tile_at(place), :] = value
             wide = value.astype(jnp.float32)
             square = wide * wide
@@ -165,10 +162,59 @@
                 part += square[:, s * TILE : (s + 1) * TILE]
             norms[pl.ds(place, 1), :] = jnp.sum(jnp.transpose(part), axis=0, keepdims=True)
             if other == 0:
-                near[tile_at(place), :] = near_refs[k][here, :]
+                near[tile_at(place), :] = own_near[k][here, :]
             elif (k, h) in LENT:
-                near[tile_at(place), :] = lent_refs[k][here, :]
-
+                near[tile_at(place), :] = lent[k][here, :]
+
+
+def pack_kernel(places, near0, near1, lent1, own0, own1, other0, other1, feats, norms, near):
+    pack_tiles(
+        (0, 1),
+        places,
+        {0: own0, 1: own1},
+        {0: other0, 1: other1},
+        {0: near0, 1: near1},
+        {1: lent1},
+        feats,
+        norms,
+        near,
+    )
+
+
+def pair_kernel(
+    places,
+    weights,
+    near2,
+    near3,
+    lent3,
+    own2,
+    own3,
+    other2,
+    other3,
+    feats_in,
+    norms_in,
+    near_in,
+    feats,
+    norms,
+    near,
+    own_out,
+    head_out,
+    grads,
+):
+    del feats_in, norms_in, near_in
+    width = feats.shape[1]
+    total, rows_here, own_valid = places[16], places[17], places[18]
+    pack_tiles(
+        (2, 3),
+        places,
+        {2: own2, 3: own3},
+        {2: other2, 3: other3},
+        {2: near2, 3: near3},
+        {3: lent3},
+        feats,
+        norms,
+        near,
+    )
     feats[tile_at(total), :] = jnp.zeros((TILE, width), jnp.bfloat16)
     norms[pl.ds(total, 1), :] = jnp.zeros((1, TILE), jnp.float32)
 
@@ -227,10 +273,7 @@
 
     own = grads[:CHUNK, :]
     row = lax.broadcasted_iota(jnp.int32, (CHUNK, 1), 0)
-    own = jnp.where(row < own_valid, own, jnp.zeros_like(own))
-    embed_out[...] = lax.dot_general(
-        own, head_ref[...], (((1,), (1,)), ((), ())), preferred_element_type=jnp.float32
-    ).astype(embed_out.dtype)
+    own_out[...] = jnp.where(row < own_valid, own, jnp.zeros_like(own))
 
 
 def gathered_body(embeddings, head_weight, gp_weights, counts):
@@ -247,6 +290,9 @@
 
     def across_cores(value):
         return lax.ppermute(value, "rep", [(0, 1), (1, 0)])
+
+    def after(value, *others):
+        return lax.optimization_barrier((value, *others))[0]
 
     smem = pl.BlockSpec(memory_space=pltpu.SMEM)
     vmem = pl.BlockSpec(memory_space=pltpu.VMEM)
@@ -271,40 +317,56 @@
         jnp.concatenate([head_mine, head_other]),
         jnp.concatenate([head_other, head_mine]),
     )
+    far0_next, weights, places = lax.optimization_barrier((far0, weights, places))
+    near3, far_head = lax.optimization_barrier((near3, far_head))
+    far2 = across_z(far0_next, 2)
     near2 = across_z(near3, 1)
-    far2 = across_z(far0, 2)
     far1 = across_x(near1)
     far3 = across_x(near3)
-    near = [embeddings, near1, near2, near3]
-    far = [far0, far1, far2, far3]
-    feats = [
-        (
-            jnp.dot(a, head_weight, preferred_element_type=jnp.float32)
-            + jnp.dot(b, far_head, preferred_element_type=jnp.float32)
-        ).astype(jnp.bfloat16)
-        for a, b in zip(near, far)
-    ]
-    feats_other = [across_cores(value) for value in feats]
-    lent = [across_cores(near1), across_cores(near3)]
-
-    embed_grad, head_part = pl.pallas_call(
+
+    def features(near, far):
+        value = jnp.dot(near, head_weight, preferred_element_type=jnp.float32)
+        value += jnp.dot(far, far_head, preferred_element_type=jnp.float32)
+        return value.astype(jnp.bfloat16)
+
+    own0, own1 = features(embeddings, far0), features(near1, far1)
+    other0, other1 = across_cores(own0), across_cores(own1)
+    lent1 = across_cores(after(near1, own1))
+    buffers = (
+        jax.ShapeDtypeStruct((18 * TILE, width), jnp.bfloat16),
+        jax.ShapeDtypeStruct((PLACES, TILE), jnp.float32),
+        jax.ShapeDtypeStruct((12 * TILE, share_cols), jnp.bfloat16),
+    )
+    packed = pl.pallas_call(
+        pack_kernel,
+        out_shape=buffers,
+        in_specs=[smem] + [vmem] * 7,
+        out_specs=(vmem,) * 3,
+        compiler_params=pltpu.CompilerParams(vmem_limit_bytes=30 * 2**20),
+    )(places, embeddings, near1, lent1, own0, own1, other0, other1)
+
+    own2, own3 = features(near2, far2), features(near3, far3)
+    other2, other3 = across_cores(own2), across_cores(own3)
+    lent3 = across_cores(after(near3, own3))
+
+    *_, own_grad, head_part = pl.pallas_call(
         pair_kernel,
-        out_shape=(
-            jax.ShapeDtypeStruct((share_rows, share_cols), jnp.bfloat16),
+        out_shape=buffers
+        + (
+            jax.ShapeDtypeStruct((share_rows, width), jnp.bfloat16),
             jax.ShapeDtypeStruct((enc_rows, width), jnp.float32),
         ),
-        in_specs=[smem] + [vmem] * 16,
-        out_specs=(vmem, vmem),
-        scratch_shapes=[
-            pltpu.VMEM((12 * TILE, share_cols), jnp.bfloat16),
-            pltpu.VMEM((18 * TILE, width), jnp.bfloat16),
-            pltpu.VMEM((PLACES, TILE), jnp.float32),
-            pltpu.VMEM((4 * CHUNK, width), jnp.bfloat16),
-        ],
+        in_specs=[smem] + [vmem] * 11,
+        out_specs=(vmem,) * 5,
+        input_output_aliases={9: 0, 10: 1, 11: 2},
+        scratch_shapes=[pltpu.VMEM((4 * CHUNK, width), jnp.bfloat16)],
         compiler_params=pltpu.CompilerParams(vmem_limit_bytes=40 * 2**20),
-    )(places, weights, head_weight, *near, *lent, *feats, *feats_other)
-    head_grad = head_part + across_cores(head_part)
-    return embed_grad, head_grad
+    )(places, weights, near2, near3, lent3, own2, own3, other2, other3, *packed)
+    head_other_part = across_cores(head_part)
+    embed_grad = lax.dot_general(
+        own_grad, head_weight, (((1,), (1,)), ((), ())), preferred_element_type=jnp.float32
+    ).astype(jnp.bfloat16)
+    return embed_grad, head_part + head_other_part
 
 
 def solution(mesh):

time: 55 us -> 43.6 us (0.79)
  waiting for transfers between devices: 22.2 us -> 11.2 us
  starting transfers between devices: 13.4 us -> 15.4 us
  Pallas kernels: 9.94 us -> 8.63 us
  local copies, waits for them, and re-layouts: 2.36 us -> 1.1 us
    ppermute x4, waiting for transfers between devices: 15.7 us -> 0.7 us  [across_z(): lax.ppermute(value, 'loop', [(i, i ^ step) for i in range(loop_size)])]
    ppermute x4, waiting for transfers between devices: 3.32 us -> 8.35 us  [across_x(): return lax.ppermute(value, 'enc', [(0, 1), (1, 0)])]
    ppermute x4, starting transfers between devices: 6.36 us -> 8.47 us  [across_z(): lax.ppermute(value, 'loop', [(i, i ^ step) for i in range(loop_size)])]
    pallas_call x1 -> x2, Pallas kernels: 8.47 us -> 7.15 us  [the longest x1 6.01 us: gathered_body(): pl.pallas_call(pair_kernel, out_shape=buffers + (jax.ShapeDtypeStruct((sh...]
    ppermute x8, waiting for transfers between devices: 3.19 us -> 2.13 us  [across_cores(): return lax.ppermute(value, 'rep', [(0, 1), (1, 0)])]
    dynamic_slice x1, local copies, waits for them, and re-layouts: 1.04 us -> 0.02 us  [gathered_body(): lax.dynamic_slice_in_dim(head_weight, rep * half, half, 0)]
    unnamed x16 -> x8, local copies, waits for them, and re-layouts: 1.31 us -> 1.08 us
    dot_general x8 -> x9, matrix products: 4.86 us -> 4.93 us  [the longest x4 2.39 us: features(): value = jnp.dot(near, head_weight, preferred_element_type=jnp.float32)]
  transfers between devices with their start and end apart: 16 -> 16, of which waited for: 7 -> 8; matrix products, arithmetic and copies ran while one was open for 9% -> 12% of each run, Pallas kernels for 3% -> 6%
where the time goes in v2:
time: 43.6 us; the launch traced here: 43.4 us
  starting transfers between devices  15.4 us (35%)
  waiting for transfers between devices  11.2 us (26%)
  Pallas kernels  8.63 us (20%)
  matrix products  4.93 us (11%)
  other arithmetic  1.33 us (3%)
  local copies, waits for them, and re-layouts  1.1 us (3%)
  between operations  0.8 us (2%)
    ppermute x4, starting transfers between devices, across_z(): lax.ppermute(value, 'loop', [(i, i ^ step) for i in range(loop_size)])  8.47 us
    ppermute x4, waiting for transfers between devices, across_x(): return lax.ppermute(value, 'enc', [(0, 1), (1, 0)])  8.35 us
    pallas_call x1, Pallas kernels, gathered_body(): pl.pallas_call(pair_kernel, out_shape=buffers + (jax.ShapeDtypeStruct((sh...  6.01 us
    ppermute x4, starting transfers between devices, across_x(): return lax.ppermute(value, 'enc', [(0, 1), (1, 0)])  5.63 us
    dot_general x4, matrix products, features(): value = jnp.dot(near, head_weight, preferred_element_type=jnp.float32)  2.39 us
    ppermute x8, waiting for transfers between devices, across_cores(): return lax.ppermute(value, 'rep', [(0, 1), (1, 0)])  2.13 us
    pallas_call x1, Pallas kernels, gathered_body(): pl.pallas_call(prep_kernel, out_shape=(jax.ShapeDtypeStruct((PLACES, TILE...  1.48 us
    dot_general x4, matrix products, features(): value += jnp.dot(far, far_head, preferred_element_type=jnp.float32)  1.47 us
  transfers between devices with their start and end apart: 16, of which 8 were waited for; matrix products, arithmetic and copies ran while one was open for 12% of the time, Pallas kernels for 6%

profile of v2, /device:TPU:0, one launch (start us, length us, event | category | flops | bytes accessed | tf_op | source)
XLA Modules:
  0.0 43.4 jit_solution(12518523194526221221)
XLA Ops:
  0.6 0.0 copy-start
  0.6 1.1 %copy-done = bf16[384,768]{1,0:T(8,128)(2,1)S(1)} copy-done((bf16[384,768]{1,0:T(8,128)(2,1)S(1)}, bf16[384,768]{1,0:T(8,128)(2,1)}, u32[]{:S(2)}) %copy-start) | copy-done | bytes 589848
  1.7 3.0 %collective-permute-start.2 = (bf16[192,768]{1,0:T(8,128)(2,1)S(1)}, bf16[192,768]{1,0:T(8,128)(2,1)S(1)}, u32[]{:S(2)}, u32[]{:S(2)}) collective-permute-start(bf16[192,768]{1,0:T(8,128)(2,1)S(1)} %constant_dynamic-slice_fusion), channel_id=1, source_target_pairs={{0,2},{2,0},{1,3},{3,1},{4,6},{6,4},{5,7},{7,5},{8,10},{10,8},{9,1... | collective-permute-start | bytes 884744 | tf_op jit(solution)/shard_map/ppermute | solution.py:289
  4.7 1.6 %collective-permute-start.10 = (bf16[256,384]{1,0:T(8,128)(2,1)}, bf16[256,384]{1,0:T(8,128)(2,1)S(1)}, u32[]{:S(2)}, u32[]{:S(2)}) collective-permute-start(bf16[256,384]{1,0:T(8,128)(2,1)} %near0.1), channel_id=1, source_target_pairs={{0,4},{4,0},{8,12},{12,8},{1,5},{5,1},{9,13},{13,9},{2,6},{6,2},{1... | collective-permute-start | bytes 589832 | tf_op jit(solution)/shard_map/ppermute | solution.py:286
  6.3 2.5 %collective-permute-start.1 = (bf16[256,384]{1,0:T(8,128)(2,1)}, bf16[256,384]{1,0:T(8,128)(2,1)S(1)}, u32[]{:S(2)}, u32[]{:S(2)}) collective-permute-start(bf16[256,384]{1,0:T(8,128)(2,1)} %near0.1), channel_id=1, source_target_pairs={{0,12},{4,8},{8,4},{12,0},{1,13},{5,9},{9,5},{13,1},{2,14},{6,10},... | collective-permute-start | bytes 589832 | tf_op jit(solution)/shard_map/ppermute | solution.py:286
  8.8 0.5 %collective-permute-start = (bf16[256,384]{1,0:T(8,128)(2,1)}, bf16[256,384]{1,0:T(8,128)(2,1)S(1)}, u32[]{:S(2)}, u32[]{:S(2)}) collective-permute-start(bf16[256,384]{1,0:T(8,128)(2,1)} %near0.1), channel_id=1, source_target_pairs={{0,2},{2,0},{1,3},{3,1},{4,6},{6,4},{5,7},{7,5},{8,10},{10,8},{9,1... | collective-permute-start | bytes 589832 | tf_op jit(solution)/shard_map/ppermute | solution.py:289
  9.3 3.2 %collective-permute-done.2 = bf16[192,768]{1,0:T(8,128)(2,1)S(1)} collective-permute-done((bf16[192,768]{1,0:T(8,128)(2,1)S(1)}, bf16[192,768]{1,0:T(8,128)(2,1)S(1)}, u32[]{:S(2)}, u32[]{:S(2)}) %collective-permute-start.2) | collective-permute-done | bytes 294944 | tf_op jit(solution)/shard_map/ppermute | solution.py:289
  12.6 0.0 collective-permute-start.3
  12.6 1.3 %fusion.9 = f32[256,768]{1,0:T(8,128)S(1)} fusion(bf16[256,384]{1,0:T(8,128)(2,1)} %near0.1, bf16[384,768]{1,0:T(8,128)(2,1)S(1)} %copy-done), kind=kOutput, calls=%fused_computation.16 | convolution fusion | flops 150994944 | bytes 1572864 | tf_op jit(solution)/shard_map/dot_general | solution.py:328
  13.9 1.5 %shard_map.59 = (f32[24,128]{1,0:T(8,128)}, s32[24]{0:T(128)}) custom-call(s32[4]{0:T(128)} %counts_ref.1, f32[16,128]{1,0:T(8,128)} %bitcast.31), custom_call_target="tpu_custom_call" | custom-call | tf_op jit(solution)/shard_map/pallas_call | solution.py:299
  15.4 0.6 %collective-permute-done = bf16[256,384]{1,0:T(8,128)(2,1)S(1)} collective-permute-done((bf16[256,384]{1,0:T(8,128)(2,1)}, bf16[256,384]{1,0:T(8,128)(2,1)S(1)}, u32[]{:S(2)}, u32[]{:S(2)}) %collective-permute-start) | collective-permute-done | bytes 196640 | tf_op jit(solution)/shard_map/ppermute | solution.py:289
  15.9 2.8 %collective-permute-start.7 = (bf16[256,384]{1,0:T(8,128)(2,1)S(1)}, bf16[256,384]{1,0:T(8,128)(2,1)S(1)}, u32[]{:S(2)}, u32[]{:S(2)}) collective-permute-start(bf16[256,384]{1,0:T(8,128)(2,1)S(1)} %collective-permute-done), channel_id=1, source_target_pairs={{0,8},{4,12},{8,0},{12,4},{1,9},{5,13},{9,1},{13,5},{2,10},{6,14},... | collective-permute-start | bytes 589832 | tf_op jit(solution)/shard_map/ppermute | solution.py:286
  18.8 0.0 collective-permute-done.10.near1
  18.8 1.5 %collective-permute-start.11 = (bf16[256,384]{1,0:T(8,128)(2,1)S(1)}, bf16[256,384]{1,0:T(8,128)(2,1)S(1)}, u32[]{:S(2)}, u32[]{:S(2)}) collective-permute-start(bf16[256,384]{1,0:T(8,128)(2,1)S(1)} %collective-permute-done.10.near1), channel_id=1, source_target_pairs={{0,2},{2,0},{1,3},{3,1},{4,6},{6,4},{5,7},{7,5},{8,10},{10,8},{9,1... | collective-permute-start | bytes 589832 | tf_op jit(solution)/shard_map/ppermute | solution.py:289
  20.3 0.4 fusion.8
  20.6 0.0 collective-permute-done.3
  20.7 0.2 maximum_select_fusion
  20.8 0.0 collective-permute-done.1.near3
  20.9 0.6 %collective-permute-start.5 = (bf16[256,384]{1,0:T(8,128)(2,1)S(1)}, bf16[256,384]{1,0:T(8,128)(2,1)S(1)}, u32[]{:S(2)}, u32[]{:S(2)}) collective-permute-start(bf16[256,384]{1,0:T(8,128)(2,1)S(1)} %collective-permute-done.1.near3), channel_id=1, source_target_pairs={{0,2},{2,0},{1,3},{3,1},{4,6},{6,4},{5,7},{7,5},{8,10},{10,8},{9,1... | collective-permute-start | bytes 589832 | tf_op jit(solution)/shard_map/ppermute | solution.py:289
  21.5 1.6 %collective-permute-start.4 = (bf16[256,384]{1,0:T(8,128)(2,1)S(1)}, bf16[256,384]{1,0:T(8,128)(2,1)S(1)}, u32[]{:S(2)}, u32[]{:S(2)}) collective-permute-start(bf16[256,384]{1,0:T(8,128)(2,1)S(1)} %collective-permute-done.1.near3), channel_id=1, source_target_pairs={{0,4},{4,0},{8,12},{12,8},{1,5},{5,1},{9,13},{13,9},{2,6},{6,2},{1... | collective-permute-start | bytes 589832 | tf_op jit(solution)/shard_map/ppermute | solution.py:286
  23.0 3.5 %collective-permute-done.11 = bf16[256,384]{1,0:T(8,128)(2,1)S(1)} collective-permute-done((bf16[256,384]{1,0:T(8,128)(2,1)S(1)}, bf16[256,384]{1,0:T(8,128)(2,1)S(1)}, u32[]{:S(2)}, u32[]{:S(2)}) %collective-permute-start.11) | collective-permute-done | bytes 196640 | tf_op jit(solution)/shard_map/ppermute | solution.py:289
  26.6 0.4 fusion.2.own1
  26.9 0.1 collective-permute-start.14
  27.0 0.5 %collective-permute-start.12 = (bf16[256,384]{1,0:T(8,128)(2,1)S(1)}, bf16[256,384]{1,0:T(8,128)(2,1)S(1)}, u32[]{:S(2)}, u32[]{:S(2)}) collective-permute-start(bf16[256,384]{1,0:T(8,128)(2,1)S(1)} %collective-permute-done.10.near1), channel_id=1, source_target_pairs={{0,1},{1,0},{2,3},{3,2},{4,5},{5,4},{6,7},{7,6},{8,9},{9,8},{10,11... | collective-permute-start | bytes 589832 | tf_op jit(solution)/shard_map/ppermute | solution.py:292
  27.5 0.4 fusion.3.own0
  27.9 0.6 %collective-permute-done.7 = bf16[256,384]{1,0:T(8,128)(2,1)S(1)} collective-permute-done((bf16[256,384]{1,0:T(8,128)(2,1)S(1)}, bf16[256,384]{1,0:T(8,128)(2,1)S(1)}, u32[]{:S(2)}, u32[]{:S(2)}) %collective-permute-start.7) | collective-permute-done | bytes 196640 | tf_op jit(solution)/shard_map/ppermute | solution.py:286
  28.5 0.4 fusion.7
  28.9 1.0 %collective-permute-done.5 = bf16[256,384]{1,0:T(8,128)(2,1)S(1)} collective-permute-done((bf16[256,384]{1,0:T(8,128)(2,1)S(1)}, bf16[256,384]{1,0:T(8,128)(2,1)S(1)}, u32[]{:S(2)}, u32[]{:S(2)}) %collective-permute-start.5) | collective-permute-done | bytes 196640 | tf_op jit(solution)/shard_map/ppermute | solution.py:289
  29.8 0.4 fusion.6
  30.2 0.4 fusion.4.own3
  30.6 0.0 copy-start.1
  30.6 0.0 copy-start.3
  30.6 0.1 collective-permute-start.9
  30.7 0.1 collective-permute-done.4.near2
  30.8 0.4 fusion.5.own2
  31.2 0.0 copy-start.2
  31.2 0.5 %collective-permute-start.8 = (bf16[256,768]{1,0:T(8,128)(2,1)S(1)}, bf16[256,768]{1,0:T(8,128)(2,1)S(1)}, u32[]{:S(2)}, u32[]{:S(2)}) collective-permute-start(bf16[256,768]{1,0:T(8,128)(2,1)S(1)} %fusion.5.own2), channel_id=1, source_target_pairs={{0,1},{1,0},{2,3},{3,2},{4,5},{5,4},{6,7},{7,6},{8,9},{9,8},{10,11... | collective-permute-start | bytes 1179656 | tf_op jit(solution)/shard_map/ppermute | solution.py:292
  31.6 0.1 collective-permute-start.6
  31.8 0.0 collective-permute-done.13.other0
  31.8 1.1 %shard_map.60 = (bf16[2304,768]{1,0:T(8,128)(2,1)S(1)}, f32[24,128]{1,0:T(8,128)S(1)}, bf16[1536,384]{1,0:T(8,128)(2,1)S(1)}) custom-call(s32[24]{0:T(128)S(1)} %copy-done.3, bf16[256,384]{1,0:T(8,128)(2,1)S(1)} %copy-done.1, bf16[256,384]{1,0:T(8,128)(2,1)S(1)} %collective-permute-done.10.near1, bf16[256,384]{1,0:T(8,128)(2,1)S(1)} %collective-permute-done.12.lent1, ...), custom_call_target="tpu_custom_call" | custom-call | tf_op jit(solution)/shard_map/pallas_call | solution.py:340
  32.9 0.4 collective-permute-done.6.lent3
  33.3 0.0 collective-permute-done.9.other3
  33.3 0.0 collective-permute-done.8.other2
  33.3 6.0 %shard_map.61 = (bf16[2304,768]{1,0:T(8,128)(2,1)S(1)}, f32[24,128]{1,0:T(8,128)S(1)}, bf16[1536,384]{1,0:T(8,128)(2,1)S(1)}, bf16[256,768]{1,0:T(8,128)(2,1)S(1)}, f32[384,768]{1,0:T(8,128)S(1)}) custom-call(s32[24]{0:T(128)S(1)} %copy-done.3, f32[24,128]{1,0:T(8,128)S(1)} %copy-done.2, ...), custom_call_target="tpu_custom_call", output_to_operand_aliasing={{0}: (9, {}), {1}: (10, {}), {2}: (11, {})} | custom-call | tf_op jit(solution)/shard_map/pallas_call | solution.py:352
  39.3 0.1 collective-permute-start.15
  39.4 1.1 %convolution_convert_fusion = bf16[256,384]{1,0:T(8,128)(2,1)} fusion(bf16[256,768]{1,0:T(8,128)(2,1)S(1)} %get-tuple-element.28, bf16[384,768]{1,0:T(8,128)(2,1)S(1)} %copy-done), kind=kOutput, calls=%fused_computation.10 | convolution fusion | flops 151093248 | bytes 1179648 | tf_op jit(solution)/shard_map/dot_general | solution.py:366
  40.4 1.8 %collective-permute-done.15 = f32[384,768]{1,0:T(8,128)S(1)} collective-permute-done((f32[384,768]{1,0:T(8,128)S(1)}, f32[384,768]{1,0:T(8,128)S(1)}, u32[]{:S(2)}, u32[]{:S(2)}) %collective-permute-start.15) | collective-permute-done | bytes 1179680 | tf_op jit(solution)/shard_map/ppermute | solution.py:292
  42.2 1.1 %add.23 = f32[384,768]{1,0:T(8,128)} add(f32[384,768]{1,0:T(8,128)S(1)} %get-tuple-element.29, f32[384,768]{1,0:T(8,128)S(1)} %collective-permute-done.15) | non-fusion elementwise | flops 294912 | bytes 3538944 | tf_op jit(solution)/shard_map/add | solution.py:369
  (7 shorter events, 0.0 us)
Async XLA Ops:
  0.6 1.1 %copy-start = (bf16[384,768]{1,0:T(8,128)(2,1)S(1)}, bf16[384,768]{1,0:T(8,128)(2,1)}, u32[]{:S(2)}) copy-start(bf16[384,768]{1,0:T(8,128)(2,1)} %param.5) | copy-start | bytes 1769476
  1.7 10.8 %collective-permute-start.2 = (bf16[192,768]{1,0:T(8,128)(2,1)S(1)}, bf16[192,768]{1,0:T(8,128)(2,1)S(1)}, u32[]{:S(2)}, u32[]{:S(2)}) collective-permute-start(bf16[192,768]{1,0:T(8,128)(2,1)S(1)} %constant_dynamic-slice_fusion), channel_id=1, source_target_pairs={{0,2},{2,0},{1,3},{3,1},{4,6},{6,4},{5,7},{7,5},{8,10},{10,8},{9,1... | collective-permute-start | bytes 884744 | tf_op jit(solution)/shard_map/ppermute | solution.py:289
  4.7 14.1 %collective-permute-start.10 = (bf16[256,384]{1,0:T(8,128)(2,1)}, bf16[256,384]{1,0:T(8,128)(2,1)S(1)}, u32[]{:S(2)}, u32[]{:S(2)}) collective-permute-start(bf16[256,384]{1,0:T(8,128)(2,1)} %near0.1), channel_id=1, source_target_pairs={{0,4},{4,0},{8,12},{12,8},{1,5},{5,1},{9,13},{13,9},{2,6},{6,2},{1... | collective-permute-start | bytes 589832 | tf_op jit(solution)/shard_map/ppermute | solution.py:286
  6.3 14.5 %collective-permute-start.1 = (bf16[256,384]{1,0:T(8,128)(2,1)}, bf16[256,384]{1,0:T(8,128)(2,1)S(1)}, u32[]{:S(2)}, u32[]{:S(2)}) collective-permute-start(bf16[256,384]{1,0:T(8,128)(2,1)} %near0.1), channel_id=1, source_target_pairs={{0,12},{4,8},{8,4},{12,0},{1,13},{5,9},{9,5},{13,1},{2,14},{6,10},... | collective-permute-start | bytes 589832 | tf_op jit(solution)/shard_map/ppermute | solution.py:286
  8.8 7.2 %collective-permute-start = (bf16[256,384]{1,0:T(8,128)(2,1)}, bf16[256,384]{1,0:T(8,128)(2,1)S(1)}, u32[]{:S(2)}, u32[]{:S(2)}) collective-permute-start(bf16[256,384]{1,0:T(8,128)(2,1)} %near0.1), channel_id=1, source_target_pairs={{0,2},{2,0},{1,3},{3,1},{4,6},{6,4},{5,7},{7,5},{8,10},{10,8},{9,1... | collective-permute-start | bytes 589832 | tf_op jit(solution)/shard_map/ppermute | solution.py:289
  12.6 8.1 %collective-permute-start.3 = (bf16[192,768]{1,0:T(8,128)(2,1)S(1)}, bf16[192,768]{1,0:T(8,128)(2,1)S(1)}, u32[]{:S(2)}, u32[]{:S(2)}) collective-permute-start(bf16[192,768]{1,0:T(8,128)(2,1)S(1)} %collective-permute-done.2), channel_id=1, source_target_pairs={{0,1},{1,0},{2,3},{3,2},{4,5},{5,4},{6,7},{7,6},{8,9},{9,8},{10,11... | collective-permute-start | bytes 884744 | tf_op jit(solution)/shard_map/ppermute | solution.py:292
  15.9 12.5 %collective-permute-start.7 = (bf16[256,384]{1,0:T(8,128)(2,1)S(1)}, bf16[256,384]{1,0:T(8,128)(2,1)S(1)}, u32[]{:S(2)}, u32[]{:S(2)}) collective-permute-start(bf16[256,384]{1,0:T(8,128)(2,1)S(1)} %collective-permute-done), channel_id=1, source_target_pairs={{0,8},{4,12},{8,0},{12,4},{1,9},{5,13},{9,1},{13,5},{2,10},{6,14},... | collective-permute-start | bytes 589832 | tf_op jit(solution)/shard_map/ppermute | solution.py:286
  18.8 7.8 %collective-permute-start.11 = (bf16[256,384]{1,0:T(8,128)(2,1)S(1)}, bf16[256,384]{1,0:T(8,128)(2,1)S(1)}, u32[]{:S(2)}, u32[]{:S(2)}) collective-permute-start(bf16[256,384]{1,0:T(8,128)(2,1)S(1)} %collective-permute-done.10.near1), channel_id=1, source_target_pairs={{0,2},{2,0},{1,3},{3,1},{4,6},{6,4},{5,7},{7,5},{8,10},{10,8},{9,1... | collective-permute-start | bytes 589832 | tf_op jit(solution)/shard_map/ppermute | solution.py:289
  20.9 9.0 %collective-permute-start.5 = (bf16[256,384]{1,0:T(8,128)(2,1)S(1)}, bf16[256,384]{1,0:T(8,128)(2,1)S(1)}, u32[]{:S(2)}, u32[]{:S(2)}) collective-permute-start(bf16[256,384]{1,0:T(8,128)(2,1)S(1)} %collective-permute-done.1.near3), channel_id=1, source_target_pairs={{0,2},{2,0},{1,3},{3,1},{4,6},{6,4},{5,7},{7,5},{8,10},{10,8},{9,1... | collective-permute-start | bytes 589832 | tf_op jit(solution)/shard_map/ppermute | solution.py:289
  21.5 9.3 %collective-permute-start.4 = (bf16[256,384]{1,0:T(8,128)(2,1)S(1)}, bf16[256,384]{1,0:T(8,128)(2,1)S(1)}, u32[]{:S(2)}, u32[]{:S(2)}) collective-permute-start(bf16[256,384]{1,0:T(8,128)(2,1)S(1)} %collective-permute-done.1.near3), channel_id=1, source_target_pairs={{0,4},{4,0},{8,12},{12,8},{1,5},{5,1},{9,13},{13,9},{2,6},{6,2},{1... | collective-permute-start | bytes 589832 | tf_op jit(solution)/shard_map/ppermute | solution.py:286
  26.9 4.8 %collective-permute-start.14 = (bf16[256,768]{1,0:T(8,128)(2,1)S(1)}, bf16[256,768]{1,0:T(8,128)(2,1)S(1)}, u32[]{:S(2)}, u32[]{:S(2)}) collective-permute-start(bf16[256,768]{1,0:T(8,128)(2,1)S(1)} %fusion.2.own1), channel_id=1, source_target_pairs={{0,1},{1,0},{2,3},{3,2},{4,5},{5,4},{6,7},{7,6},{8,9},{9,8},{10,11... | collective-permute-start | bytes 1179656 | tf_op jit(solution)/shard_map/ppermute | solution.py:292
  27.0 4.6 %collective-permute-start.12 = (bf16[256,384]{1,0:T(8,128)(2,1)S(1)}, bf16[256,384]{1,0:T(8,128)(2,1)S(1)}, u32[]{:S(2)}, u32[]{:S(2)}) collective-permute-start(bf16[256,384]{1,0:T(8,128)(2,1)S(1)} %collective-permute-done.10.near1), channel_id=1, source_target_pairs={{0,1},{1,0},{2,3},{3,2},{4,5},{5,4},{6,7},{7,6},{8,9},{9,8},{10,11... | collective-permute-start | bytes 589832 | tf_op jit(solution)/shard_map/ppermute | solution.py:292
  28.5 3.3 %collective-permute-start.13 = (bf16[256,768]{1,0:T(8,128)(2,1)S(1)}, bf16[256,768]{1,0:T(8,128)(2,1)S(1)}, u32[]{:S(2)}, u32[]{:S(2)}) collective-permute-start(bf16[256,768]{1,0:T(8,128)(2,1)S(1)} %fusion.3.own0), channel_id=1, source_target_pairs={{0,1},{1,0},{2,3},{3,2},{4,5},{5,4},{6,7},{7,6},{8,9},{9,8},{10,11... | collective-permute-start | bytes 1179656 | tf_op jit(solution)/shard_map/ppermute | solution.py:292
  30.6 1.2 %copy-start.1 = (bf16[256,384]{1,0:T(8,128)(2,1)S(1)}, bf16[256,384]{1,0:T(8,128)(2,1)}, u32[]{:S(2)}) copy-start(bf16[256,384]{1,0:T(8,128)(2,1)} %near0.1) | copy-start | bytes 589828
  30.6 1.2 %copy-start.3 = (s32[24]{0:T(128)S(1)}, s32[24]{0:T(128)}, u32[]{:S(2)}) copy-start(s32[24]{0:T(128)} %get-tuple-element.18.places) | copy-start | bytes 292
  30.6 2.7 %collective-permute-start.9 = (bf16[256,768]{1,0:T(8,128)(2,1)S(1)}, bf16[256,768]{1,0:T(8,128)(2,1)S(1)}, u32[]{:S(2)}, u32[]{:S(2)}) collective-permute-start(bf16[256,768]{1,0:T(8,128)(2,1)S(1)} %fusion.4.own3), channel_id=1, source_target_pairs={{0,1},{1,0},{2,3},{3,2},{4,5},{5,4},{6,7},{7,6},{8,9},{9,8},{10,11... | collective-permute-start | bytes 1179656 | tf_op jit(solution)/shard_map/ppermute | solution.py:292
  31.2 2.1 %copy-start.2 = (f32[24,128]{1,0:T(8,128)S(1)}, f32[24,128]{1,0:T(8,128)}, u32[]{:S(2)}) copy-start(f32[24,128]{1,0:T(8,128)} %get-tuple-element.19.weights) | copy-start | bytes 36868
  31.2 2.1 %collective-permute-start.8 = (bf16[256,768]{1,0:T(8,128)(2,1)S(1)}, bf16[256,768]{1,0:T(8,128)(2,1)S(1)}, u32[]{:S(2)}, u32[]{:S(2)}) collective-permute-start(bf16[256,768]{1,0:T(8,128)(2,1)S(1)} %fusion.5.own2), channel_id=1, source_target_pairs={{0,1},{1,0},{2,3},{3,2},{4,5},{5,4},{6,7},{7,6},{8,9},{9,8},{10,11... | collective-permute-start | bytes 1179656 | tf_op jit(solution)/shard_map/ppermute | solution.py:292
  31.6 1.6 %collective-permute-start.6 = (bf16[256,384]{1,0:T(8,128)(2,1)S(1)}, bf16[256,384]{1,0:T(8,128)(2,1)S(1)}, u32[]{:S(2)}, u32[]{:S(2)}) collective-permute-start(bf16[256,384]{1,0:T(8,128)(2,1)S(1)} %collective-permute-done.1.near3), channel_id=1, source_target_pairs={{0,1},{1,0},{2,3},{3,2},{4,5},{5,4},{6,7},{7,6},{8,9},{9,8},{10,11... | collective-permute-start | bytes 589832 | tf_op jit(solution)/shard_map/ppermute | solution.py:292
  39.3 2.9 %collective-permute-start.15 = (f32[384,768]{1,0:T(8,128)S(1)}, f32[384,768]{1,0:T(8,128)S(1)}, u32[]{:S(2)}, u32[]{:S(2)}) collective-permute-start(f32[384,768]{1,0:T(8,128)S(1)} %get-tuple-element.29), channel_id=1, source_target_pairs={{0,1},{1,0},{2,3},{3,2},{4,5},{5,4},{6,7},{7,6},{8,9},{9,8},{10,11... | collective-permute-start | bytes 3538952 | tf_op jit(solution)/shard_map/ppermute | solution.py:292
